TPU v7x, 128 devices: a whole 4x4x4 slice. The times are simulated.
128 devices in a mesh: row: 4 (over y), col: 16 (over x, z_hi, core), depth: 2 (over z_lo).
Axes of the slice: x: 4, y: 4, z: 4 (z_hi: 2, z_lo: 2; z = z_hi * 2 + z_lo), core: 2. Of those that a mesh axis runs over, the one named last changes fastest.
Arguments:
- values: bfloat16 [800, 80, 128, 128], P(('row', 'depth'), 'col'), may hold values from -2 to 2
- pattern: int32 [800, 80], P(('row', 'depth'), 'col'), may hold values from 0 to 49, as said below
- branch_flag: int32 [40], replicated, may hold values from 0 to 1, as said below
Outputs:
- purified: bfloat16 [40, 80, 128, 128], P(('row', 'depth'), 'col')
Inputs may be any that keep to these rules, and one draw needn't show every extreme that they name: `pattern`: block columns fall into classes with 5 members in every column panel; block (i, j) is nonzero exactly when i and j are in the same class, and the 5 slots of a block row in panel c list, in no particular order, the distinct panel-local indices of the members of its class in that panel. `branch_flag`: exactly half of the entries, rounded down, are 1; the rest are 0.
All inputs are finite; a program needn't handle non-finite values.
Results may differ from a plain program's by a relative error of at most 0.001.
Values may be sent and summed in bfloat16 or wider, within the bound.
A program may use at most 128 MiB of HBM per device.

v0:
```python
import jax
import jax.numpy as jnp
from jax import lax
from jax.sharding import PartitionSpec as P

SLAB_DEV = 5


def broadcast(block, axis, holder):
    block = jnp.where(lax.axis_index(axis) == holder, block, jnp.zeros_like(block))
    return lax.psum(block, axis)


def body(values, pattern, branch_flag):
    groups = lax.axis_size(("row", "depth"))
    shard_index = lax.axis_index(("row", "depth"))
    panels = lax.axis_size("col")
    rows_here = values.shape[0]
    slot_count = values.shape[1]
    block_size = values.shape[2]
    total_rows = rows_here * groups
    panel_cols = total_rows // panels
    stride = rows_here // SLAB_DEV
    panel_count = max(1, rows_here // panel_cols)
    first_panel = shard_index * rows_here // panel_cols
    mine_vals = values[::stride]
    mine_cols = pattern[::stride]
    slab_vals, slab_cols = (
        lax.all_gather(mine_vals, ("row", "depth"), axis=0, tiled=True),
        lax.all_gather(mine_cols, ("row", "depth"), axis=0, tiled=True),
    )
    piece_vals = []
    piece_cols = []
    for offset in range(panel_count):
        root_panel = first_panel + offset
        got_vals, got_cols = (
            broadcast(slab_vals, "col", root_panel),
            broadcast(slab_cols, "col", root_panel),
        )
        piece_vals.append(got_vals)
        piece_cols.append(got_cols + root_panel * panel_cols)
    left_vals = jnp.concatenate(piece_vals, 1)
    left_cols = jnp.concatenate(piece_cols, 1)
    slab_total = left_vals.shape[0]
    left_slots = left_vals.shape[1]
    local_rows = left_cols - shard_index * rows_here
    inside = (local_rows >= 0) & (local_rows < rows_here)
    local_rows = jnp.clip(local_rows, 0, rows_here - 1).astype(jnp.int32)
    left_vals = jnp.where(inside[:, :, None, None], left_vals, jnp.zeros((), left_vals.dtype))
    right_cols = pattern[local_rows]
    match = right_cols[:, :, None, :] == slab_cols[:, None, :, None]
    present = jnp.any(match, axis=3)
    slot_iota = lax.broadcasted_iota(jnp.int32, match.shape, 3)
    chosen = jnp.sum(jnp.where(match, slot_iota, 0), axis=3)
    group_rows = slab_total // groups

    def group_product(items):
        block_vals, row_index, slot_index, live = items
        picked = values[row_index[:, :, None], slot_index]
        picked = jnp.where(live[:, :, :, None, None], picked, jnp.zeros((), picked.dtype))
        return jnp.einsum(
            "ilab,ilmbc->imac", block_vals, picked, preferred_element_type=jnp.float32
        )

    partial_terms = lax.map(
        group_product,
        (
            left_vals.reshape(groups, group_rows, left_slots, block_size, block_size),
            local_rows.reshape(groups, group_rows, left_slots),
            chosen.reshape(groups, group_rows, left_slots, slot_count),
            present.reshape(groups, group_rows, left_slots, slot_count),
        ),
    )
    partial_terms = partial_terms.reshape(slab_total, slot_count, block_size, block_size)
    summed = lax.psum_scatter(partial_terms, ("row", "depth"), scatter_dimension=0, tiled=True)
    own_count = mine_vals.shape[0]
    own_flags = lax.dynamic_slice_in_dim(branch_flag, shard_index * own_count, own_count)
    own = mine_vals.astype(jnp.float32)
    result = jnp.where(own_flags[:, None, None, None] == 1, summed, 2.0 * own - summed)
    return result.astype(jnp.bfloat16)


def solution(mesh):
    in_specs = (P(("row", "depth"), "col", None, None), P(("row", "depth"), "col"), P())
    out_specs = P(("row", "depth"), "col", None, None)
    return jax.shard_map(body, mesh=mesh, in_specs=in_specs, out_specs=out_specs, check_vma=False)
```

profile of v0, /device:TPU:1, one launch (start us, length us, event | category | flops | bytes accessed | tf_op | source)
XLA Modules:
  0.0 1057.2 jit_solution(11381887055578751937)
XLA Ops:
  8.8 137.5 %all-gather.3.cloned.1.call-done = bf16[40,5,128,128]{3,2,1,0:T(8,128)(2,1)} async-done(((bf16[5,5,128,128]{3,2,1,0:T(8,128)(2,1)}), bf16[40,5,128,128]{3,2,1,0:T(8,128)(2,1)}) %all-gather.3.cloned.1.call-update) | async-done | bytes 6553616 | tf_op jit(solution)/shard_map/all_gather | solution.py:29
  146.2 8.4 broadcast_select_fusion.1
  155.4 30.0 %all-gather = s32[8,5,5]{2,1,0:T(8,128)S(1)} all-gather(s32[1,5,5]{2,1,0:T(8,128)S(1)} %bitcast.59), channel_id=1, replica_groups=mesh['row'=4,'col'=16,'depth'=2] {'row','depth'}, dimensions={0}, use_global_device_ids=true | all-gather | bytes 900 | tf_op jit(solution)/shard_map/all_gather | solution.py:30
  185.5 15.9 %all-reduce = (s32[40,5]{0,1:T(8,128)S(1)}, s32[40,5]{0,1:T(8,128)S(1)}) all-reduce(s32[40,5]{0,1:T(8,128)S(1)} %get-tuple-element.92, s32[40,5]{0,1:T(8,128)S(1)} %get-tuple-element.91), channel_id=1, replica_groups=mesh['row'=4,'col'=16,'depth'=2] {'col'}, use_global_device_ids=true, to_apply=%region_1.2 | all-reduce | flops 400 | bytes 3200 | tf_op jit(solution)/shard_map/psum | solution.py:11
  204.9 248.1 %all-reduce.4.cloned.1.call-done = (bf16[8,5,5,128,128]{4,3,2,1,0:T(8,128)(2,1)}, bf16[8,5,5,128,128]{4,3,2,1,0:T(8,128)(2,1)}) async-done(((bf16[8,5,5,128,128]{4,3,2,1,0:T(8,128)(2,1)}, bf16[8,5,5,128,128]{4,3,2,1,0:T(8,128)(2,1)}), (bf16[8,5,5,128,128]{4,3,2,1,0:T(8,128)(2,1)}, bf16[8,5,5,128,128]{4,3,2,1,0:T(8,128)(2,1)})) %all-reduce.4.cloned.1.call-update) | async-done | bytes 13107216 | tf_op jit(solution)/shard_map/psum | solution.py:11
  453.0 10.1 maximum_select_fusion
  463.1 327.5 %while.10 = (s32[]{:T(128)}, f32[8,5,5,128,128]{4,3,2,1,0:T(8,128)}, pred[8,5,10,5]{2,3,1,0:T(8,128)(4,1)S(1)}, s32[8,5,10]{2,1,0:T(8,128)S(1)}, s32[8,5,10,5]{3...) while((s32[]{:T(128)}, ...), condition=%wide.region_7.8_spmd, body=%wide.region_6.7_spmd.sunk | while | flops 1052673728 | bytes 50798872 | solution.py:65
  464.1 17.9 %gather_fusion = bf16[250,128,128]{2,1,0:T(8,128)(2,1)} fusion(bf16[100,5,128,128]{3,2,1,0:T(8,128)(2,1)} %get-tuple-element.159, s32[250]{0:T(256)S(1)} %reshape.163), kind=kCustom, calls=%fused_computation.clone.1 | custom fusion | bytes 16386000 | tf_op jit(solution)/shard_map/while/body/eval_jaxpr/gather | solution.py:59
  482.1 12.8 %copy.65 = bf16[5,10,5,128,128]{3,4,1,2,0:T(8,128)(2,1)} copy(bf16[5,10,5,128,128]{4,3,2,1,0:T(8,128)(2,1)} %bitcast.52) | data formatting | bytes 16384000 | tf_op jit(solution)/shard_map/while/body/eval_jaxpr/gather | solution.py:59
  494.9 6.1 fusion.31
  505.0 17.9 %gather_fusion = bf16[250,128,128]{2,1,0:T(8,128)(2,1)} fusion(bf16[100,5,128,128]{3,2,1,0:T(8,128)(2,1)} %get-tuple-element.159, s32[250]{0:T(256)S(1)} %reshape.163), kind=kCustom, calls=%fused_computation.clone.1 | custom fusion | bytes 16386000 | tf_op jit(solution)/shard_map/while/body/eval_jaxpr/gather | solution.py:59
  523.0 12.8 %copy.65 = bf16[5,10,5,128,128]{3,4,1,2,0:T(8,128)(2,1)} copy(bf16[5,10,5,128,128]{4,3,2,1,0:T(8,128)(2,1)} %bitcast.52) | data formatting | bytes 16384000 | tf_op jit(solution)/shard_map/while/body/eval_jaxpr/gather | solution.py:59
  535.8 6.1 fusion.31
  546.0 17.9 %gather_fusion = bf16[250,128,128]{2,1,0:T(8,128)(2,1)} fusion(bf16[100,5,128,128]{3,2,1,0:T(8,128)(2,1)} %get-tuple-element.159, s32[250]{0:T(256)S(1)} %reshape.163), kind=kCustom, calls=%fused_computation.clone.1 | custom fusion | bytes 16386000 | tf_op jit(solution)/shard_map/while/body/eval_jaxpr/gather | solution.py:59
  563.9 12.8 %copy.65 = bf16[5,10,5,128,128]{3,4,1,2,0:T(8,128)(2,1)} copy(bf16[5,10,5,128,128]{4,3,2,1,0:T(8,128)(2,1)} %bitcast.52) | data formatting | bytes 16384000 | tf_op jit(solution)/shard_map/while/body/eval_jaxpr/gather | solution.py:59
  576.8 6.1 fusion.31
  586.9 17.9 %gather_fusion = bf16[250,128,128]{2,1,0:T(8,128)(2,1)} fusion(bf16[100,5,128,128]{3,2,1,0:T(8,128)(2,1)} %get-tuple-element.159, s32[250]{0:T(256)S(1)} %reshape.163), kind=kCustom, calls=%fused_computation.clone.1 | custom fusion | bytes 16386000 | tf_op jit(solution)/shard_map/while/body/eval_jaxpr/gather | solution.py:59
  604.8 12.8 %copy.65 = bf16[5,10,5,128,128]{3,4,1,2,0:T(8,128)(2,1)} copy(bf16[5,10,5,128,128]{4,3,2,1,0:T(8,128)(2,1)} %bitcast.52) | data formatting | bytes 16384000 | tf_op jit(solution)/shard_map/while/body/eval_jaxpr/gather | solution.py:59
  617.7 6.1 fusion.31
  627.8 17.9 %gather_fusion = bf16[250,128,128]{2,1,0:T(8,128)(2,1)} fusion(bf16[100,5,128,128]{3,2,1,0:T(8,128)(2,1)} %get-tuple-element.159, s32[250]{0:T(256)S(1)} %reshape.163), kind=kCustom, calls=%fused_computation.clone.1 | custom fusion | bytes 16386000 | tf_op jit(solution)/shard_map/while/body/eval_jaxpr/gather | solution.py:59
  645.8 12.8 %copy.65 = bf16[5,10,5,128,128]{3,4,1,2,0:T(8,128)(2,1)} copy(bf16[5,10,5,128,128]{4,3,2,1,0:T(8,128)(2,1)} %bitcast.52) | data formatting | bytes 16384000 | tf_op jit(solution)/shard_map/while/body/eval_jaxpr/gather | solution.py:59
  658.6 6.1 fusion.31
  668.7 17.9 %gather_fusion = bf16[250,128,128]{2,1,0:T(8,128)(2,1)} fusion(bf16[100,5,128,128]{3,2,1,0:T(8,128)(2,1)} %get-tuple-element.159, s32[250]{0:T(256)S(1)} %reshape.163), kind=kCustom, calls=%fused_computation.clone.1 | custom fusion | bytes 16386000 | tf_op jit(solution)/shard_map/while/body/eval_jaxpr/gather | solution.py:59
  686.7 12.8 %copy.65 = bf16[5,10,5,128,128]{3,4,1,2,0:T(8,128)(2,1)} copy(bf16[5,10,5,128,128]{4,3,2,1,0:T(8,128)(2,1)} %bitcast.52) | data formatting | bytes 16384000 | tf_op jit(solution)/shard_map/while/body/eval_jaxpr/gather | solution.py:59
  699.5 6.1 fusion.31
  709.7 17.9 %gather_fusion = bf16[250,128,128]{2,1,0:T(8,128)(2,1)} fusion(bf16[100,5,128,128]{3,2,1,0:T(8,128)(2,1)} %get-tuple-element.159, s32[250]{0:T(256)S(1)} %reshape.163), kind=kCustom, calls=%fused_computation.clone.1 | custom fusion | bytes 16386000 | tf_op jit(solution)/shard_map/while/body/eval_jaxpr/gather | solution.py:59
  727.6 12.8 %copy.65 = bf16[5,10,5,128,128]{3,4,1,2,0:T(8,128)(2,1)} copy(bf16[5,10,5,128,128]{4,3,2,1,0:T(8,128)(2,1)} %bitcast.52) | data formatting | bytes 16384000 | tf_op jit(solution)/shard_map/while/body/eval_jaxpr/gather | solution.py:59
  740.5 6.1 fusion.31
  750.6 17.9 %gather_fusion = bf16[250,128,128]{2,1,0:T(8,128)(2,1)} fusion(bf16[100,5,128,128]{3,2,1,0:T(8,128)(2,1)} %get-tuple-element.159, s32[250]{0:T(256)S(1)} %reshape.163), kind=kCustom, calls=%fused_computation.clone.1 | custom fusion | bytes 16386000 | tf_op jit(solution)/shard_map/while/body/eval_jaxpr/gather | solution.py:59
  768.5 12.8 %copy.65 = bf16[5,10,5,128,128]{3,4,1,2,0:T(8,128)(2,1)} copy(bf16[5,10,5,128,128]{4,3,2,1,0:T(8,128)(2,1)} %bitcast.52) | data formatting | bytes 16384000 | tf_op jit(solution)/shard_map/while/body/eval_jaxpr/gather | solution.py:59
  781.4 6.1 fusion.31
  791.4 256.4 %reduce-scatter.2.cloned.1.call-done = f32[5,5,128,128]{3,2,1,0:T(8,128)} async-done(((f32[40,5,128,128]{3,2,1,0:T(8,128)}), f32[5,5,128,128]{3,2,1,0:T(8,128)}) %reduce-scatter.2.cloned.1.call-update) | async-done | bytes 1638416 | tf_op jit(solution)/shard_map/reduce_scatter | solution.py:75
  (86 shorter events, 42.6 us)
Async XLA Ops:
  6.5 139.7 %all-gather.3.cloned.1.call-start = ((), (), s32[]{:S(2)}) async-start(), calls=%async_computation.1 | async-start | bytes 7372800 | tf_op jit(solution)/shard_map/all_gather | solution.py:29
  8.7 444.4 %all-reduce.4.cloned.1.call-start = ((), (), s32[]{:S(2)}) async-start(), calls=%async_computation.3 | async-start | bytes 26214400 | tf_op jit(solution)/shard_map/psum | solution.py:11
  154.6 0.7 copy-start
  154.6 893.1 %reduce-scatter.2.cloned.1.call-start = ((), (), s32[]{:S(2)}) async-start(), calls=%async_computation.2 | async-start | bytes 14745600 | tf_op jit(solution)/shard_map/reduce_scatter | solution.py:75
  790.6 0.7 copy-start.1
Sparse Core Ops, SparseCore 0:
  9.0 137.1 all-gather.2
  154.8 298.2 all-reduce.3
  790.8 256.9 reduce-scatter.1
where the time goes:
time: 1060 us
  waiting for transfers between devices  642 us (61%)
  local copies, waits for them, and re-layouts  278 us (26%)
  matrix products  48.7 us (5%)
  blocking collectives  45.9 us (4%)
  other arithmetic  28.6 us (3%)
  between operations  13.2 us (1%)
    reduce_scatter x1, waiting for transfers between devices, body(): lax.psum_scatter(partial_terms, ('row', 'depth'), scatter_dimension=0, ti...  256 us
    psum x1, waiting for transfers between devices, broadcast(): return lax.psum(block, axis)  248 us
    gather x16, local copies, waits for them, and re-layouts, group_product(): picked = values[row_index[:, :, None], slot_index]  246 us
    all_gather x1, waiting for transfers between devices, body(): lax.all_gather(mine_vals, ('row', 'depth'), axis=0, tiled=True)  137 us
    dot_general x8, matrix products, group_product(): jnp.einsum('ilab,ilmbc->imac', block_vals, picked, preferred_element_type...  48.7 us
    all_gather x1, blocking collectives, body(): lax.all_gather(mine_cols, ('row', 'depth'), axis=0, tiled=True)  30 us
    dynamic_update_slice x16, local copies, waits for them, and re-layouts, body(): lax.map(group_product, (left_vals.reshape(groups, group_rows, left_slots,...  24.6 us
  transfers between devices with their start and end apart: 3, of which 3 were waited for; matrix products, arithmetic and copies ran while one was open for 0% of the time, Pallas kernels for 0%

commit v1 on v0

--- a/solution.py
+++ b/solution.py
@@ -25,8 +25,17 @@
     first_panel = shard_index * rows_here // panel_cols
     mine_vals = values[::stride]
     mine_cols = pattern[::stride]
+    clusters_obtain = lambda page, bus_axis, dim_i: jnp.concatenate(
+        jax.lax.all_to_all(
+            jnp.stack([page for _ in range(jax.lax.psum(1, axis_name=bus_axis))]),
+            axis_name=bus_axis,
+            split_axis=0,
+            concat_axis=0,
+        ),
+        axis=dim_i,
+    )
     slab_vals, slab_cols = (
-        lax.all_gather(mine_vals, ("row", "depth"), axis=0, tiled=True),
+        clusters_obtain(mine_vals, ("row", "depth"), 0),
         lax.all_gather(mine_cols, ("row", "depth"), axis=0, tiled=True),
     )
     piece_vals = []

time: 1060 us -> 1020 us (0.962)
  waiting for transfers between devices: 642 us -> 595 us
    all_gather x1 -> x0, waiting for transfers between devices: 137 us -> none  [body(): lax.all_gather(mine_vals, ('row', 'depth'), axis=0, tiled=True)]
    all_to_all x0 -> x1, waiting for transfers between devices: none -> 90.5 us  [body(): jax.lax.all_to_all(jnp.stack([page for _ in range(jax.lax.psum(1, axis_na...]
where the time goes in v1:
time: 1020 us
  waiting for transfers between devices  595 us (58%)
  local copies, waits for them, and re-layouts  282 us (28%)
  matrix products  48.7 us (5%)
  blocking collectives  44.5 us (4%)
  other arithmetic  28.6 us (3%)
  between operations  13.5 us (1%)
    reduce_scatter x1, waiting for transfers between devices, body(): lax.psum_scatter(partial_terms, ('row', 'depth'), scatter_dimension=0, ti...  256 us
    psum x1, waiting for transfers between devices, broadcast(): return lax.psum(block, axis)  248 us
    gather x16, local copies, waits for them, and re-layouts, group_product(): picked = values[row_index[:, :, None], slot_index]  246 us
    all_to_all x1, waiting for transfers between devices, body(): jax.lax.all_to_all(jnp.stack([page for _ in range(jax.lax.psum(1, axis_na...  90.5 us
    dot_general x8, matrix products, group_product(): jnp.einsum('ilab,ilmbc->imac', block_vals, picked, preferred_element_type...  48.7 us
    all_gather x1, blocking collectives, body(): lax.all_gather(mine_cols, ('row', 'depth'), axis=0, tiled=True)  28.3 us
    dynamic_update_slice x16, local copies, waits for them, and re-layouts, body(): lax.map(group_product, (left_vals.reshape(groups, group_rows, left_slots,...  24.6 us
  transfers between devices with their start and end apart: 3, of which 3 were waited for; matrix products, arithmetic and copies ran while one was open for 0% of the time, Pallas kernels for 0%

profile of v1, /device:TPU:1, one launch (start us, length us, event | category | flops | bytes accessed | tf_op | source)
XLA Modules:
  0.0 1018.7 jit_solution(11538768025000125757)
XLA Ops:
  12.2 6.4 all-to-all-start
  18.6 90.5 %all-to-all-done = bf16[8,5,5,128,128]{4,3,2,1,0:T(8,128)(2,1)} async-done(((bf16[8,5,5,128,128]{4,3,2,1,0:T(8,128)(2,1)}), bf16[8,5,5,128,128]{4,3,2,1,0:T(8,128)(2,1)}, u32[]{:S(2)}, u32[]{:S(2)}) %all-to-all-start) | async-done | bytes 6553632 | tf_op jit(solution)/shard_map/all_to_all | solution.py:29
  109.1 8.4 broadcast_select_fusion.1
  118.3 28.3 %all-gather = s32[8,5,5]{2,1,0:T(8,128)S(1)} all-gather(s32[1,5,5]{2,1,0:T(8,128)S(1)} %bitcast.55), channel_id=1, replica_groups=mesh['row'=4,'col'=16,'depth'=2] {'row','depth'}, dimensions={0}, use_global_device_ids=true | all-gather | bytes 900 | tf_op jit(solution)/shard_map/all_gather | solution.py:39
  146.7 16.2 %all-reduce = (s32[40,5]{0,1:T(8,128)S(1)}, s32[40,5]{0,1:T(8,128)S(1)}) all-reduce(s32[40,5]{0,1:T(8,128)S(1)} %get-tuple-element.92, s32[40,5]{0,1:T(8,128)S(1)} %get-tuple-element.91), channel_id=1, replica_groups=mesh['row'=4,'col'=16,'depth'=2] {'col'}, use_global_device_ids=true, to_apply=%region_1.2 | all-reduce | flops 400 | bytes 3200 | tf_op jit(solution)/shard_map/psum | solution.py:11
  166.4 247.9 %all-reduce.4.cloned.1.call-done = (bf16[8,5,5,128,128]{4,3,2,1,0:T(8,128)(2,1)}, bf16[8,5,5,128,128]{4,3,2,1,0:T(8,128)(2,1)}) async-done(((bf16[8,5,5,128,128]{4,3,2,1,0:T(8,128)(2,1)}, bf16[8,5,5,128,128]{4,3,2,1,0:T(8,128)(2,1)}), (bf16[8,5,5,128,128]{4,3,2,1,0:T(8,128)(2,1)}, bf16[8,5,5,128,128]{4,3,2,1,0:T(8,128)(2,1)})) %all-reduce.4.cloned.1.call-update) | async-done | bytes 13107216 | tf_op jit(solution)/shard_map/psum | solution.py:11
  414.2 10.1 maximum_select_fusion
  424.3 327.5 %while.10 = (s32[]{:T(128)}, f32[8,5,5,128,128]{4,3,2,1,0:T(8,128)}, pred[8,5,10,5]{2,3,1,0:T(8,128)(4,1)S(1)}, s32[8,5,10]{2,1,0:T(8,128)S(1)}, s32[8,5,10,5]{3...) while((s32[]{:T(128)}, ...), condition=%wide.region_7.8_spmd, body=%wide.region_6.7_spmd.sunk | while | flops 1052673728 | bytes 50798872 | solution.py:74
  425.3 17.9 %gather_fusion = bf16[250,128,128]{2,1,0:T(8,128)(2,1)} fusion(bf16[100,5,128,128]{3,2,1,0:T(8,128)(2,1)} %get-tuple-element.159, s32[250]{0:T(256)S(1)} %reshape.174), kind=kCustom, calls=%fused_computation.clone.1 | custom fusion | bytes 16386000 | tf_op jit(solution)/shard_map/while/body/eval_jaxpr/gather | solution.py:68
  443.2 12.8 %copy.65 = bf16[5,10,5,128,128]{3,4,1,2,0:T(8,128)(2,1)} copy(bf16[5,10,5,128,128]{4,3,2,1,0:T(8,128)(2,1)} %bitcast.50) | data formatting | bytes 16384000 | tf_op jit(solution)/shard_map/while/body/eval_jaxpr/gather | solution.py:68
  456.1 6.1 fusion.31
  466.2 17.9 %gather_fusion = bf16[250,128,128]{2,1,0:T(8,128)(2,1)} fusion(bf16[100,5,128,128]{3,2,1,0:T(8,128)(2,1)} %get-tuple-element.159, s32[250]{0:T(256)S(1)} %reshape.174), kind=kCustom, calls=%fused_computation.clone.1 | custom fusion | bytes 16386000 | tf_op jit(solution)/shard_map/while/body/eval_jaxpr/gather | solution.py:68
  484.2 12.8 %copy.65 = bf16[5,10,5,128,128]{3,4,1,2,0:T(8,128)(2,1)} copy(bf16[5,10,5,128,128]{4,3,2,1,0:T(8,128)(2,1)} %bitcast.50) | data formatting | bytes 16384000 | tf_op jit(solution)/shard_map/while/body/eval_jaxpr/gather | solution.py:68
  497.0 6.1 fusion.31
  507.2 17.9 %gather_fusion = bf16[250,128,128]{2,1,0:T(8,128)(2,1)} fusion(bf16[100,5,128,128]{3,2,1,0:T(8,128)(2,1)} %get-tuple-element.159, s32[250]{0:T(256)S(1)} %reshape.174), kind=kCustom, calls=%fused_computation.clone.1 | custom fusion | bytes 16386000 | tf_op jit(solution)/shard_map/while/body/eval_jaxpr/gather | solution.py:68
  525.1 12.8 %copy.65 = bf16[5,10,5,128,128]{3,4,1,2,0:T(8,128)(2,1)} copy(bf16[5,10,5,128,128]{4,3,2,1,0:T(8,128)(2,1)} %bitcast.50) | data formatting | bytes 16384000 | tf_op jit(solution)/shard_map/while/body/eval_jaxpr/gather | solution.py:68
  537.9 6.1 fusion.31
  548.1 17.9 %gather_fusion = bf16[250,128,128]{2,1,0:T(8,128)(2,1)} fusion(bf16[100,5,128,128]{3,2,1,0:T(8,128)(2,1)} %get-tuple-element.159, s32[250]{0:T(256)S(1)} %reshape.174), kind=kCustom, calls=%fused_computation.clone.1 | custom fusion | bytes 16386000 | tf_op jit(solution)/shard_map/while/body/eval_jaxpr/gather | solution.py:68
  566.0 12.8 %copy.65 = bf16[5,10,5,128,128]{3,4,1,2,0:T(8,128)(2,1)} copy(bf16[5,10,5,128,128]{4,3,2,1,0:T(8,128)(2,1)} %bitcast.50) | data formatting | bytes 16384000 | tf_op jit(solution)/shard_map/while/body/eval_jaxpr/gather | solution.py:68
  578.9 6.1 fusion.31
  589.0 17.9 %gather_fusion = bf16[250,128,128]{2,1,0:T(8,128)(2,1)} fusion(bf16[100,5,128,128]{3,2,1,0:T(8,128)(2,1)} %get-tuple-element.159, s32[250]{0:T(256)S(1)} %reshape.174), kind=kCustom, calls=%fused_computation.clone.1 | custom fusion | bytes 16386000 | tf_op jit(solution)/shard_map/while/body/eval_jaxpr/gather | solution.py:68
  606.9 12.8 %copy.65 = bf16[5,10,5,128,128]{3,4,1,2,0:T(8,128)(2,1)} copy(bf16[5,10,5,128,128]{4,3,2,1,0:T(8,128)(2,1)} %bitcast.50) | data formatting | bytes 16384000 | tf_op jit(solution)/shard_map/while/body/eval_jaxpr/gather | solution.py:68
  619.8 6.1 fusion.31
  629.9 17.9 %gather_fusion = bf16[250,128,128]{2,1,0:T(8,128)(2,1)} fusion(bf16[100,5,128,128]{3,2,1,0:T(8,128)(2,1)} %get-tuple-element.159, s32[250]{0:T(256)S(1)} %reshape.174), kind=kCustom, calls=%fused_computation.clone.1 | custom fusion | bytes 16386000 | tf_op jit(solution)/shard_map/while/body/eval_jaxpr/gather | solution.py:68
  647.9 12.8 %copy.65 = bf16[5,10,5,128,128]{3,4,1,2,0:T(8,128)(2,1)} copy(bf16[5,10,5,128,128]{4,3,2,1,0:T(8,128)(2,1)} %bitcast.50) | data formatting | bytes 16384000 | tf_op jit(solution)/shard_map/while/body/eval_jaxpr/gather | solution.py:68
  670.9 17.9 %gather_fusion = bf16[250,128,128]{2,1,0:T(8,128)(2,1)} fusion(bf16[100,5,128,128]{3,2,1,0:T(8,128)(2,1)} %get-tuple-element.159, s32[250]{0:T(256)S(1)} %reshape.174), kind=kCustom, calls=%fused_computation.clone.1 | custom fusion | bytes 16386000 | tf_op jit(solution)/shard_map/while/body/eval_jaxpr/gather | solution.py:68
  688.8 12.8 %copy.65 = bf16[5,10,5,128,128]{3,4,1,2,0:T(8,128)(2,1)} copy(bf16[5,10,5,128,128]{4,3,2,1,0:T(8,128)(2,1)} %bitcast.50) | data formatting | bytes 16384000 | tf_op jit(solution)/shard_map/while/body/eval_jaxpr/gather | solution.py:68
  701.7 6.1 fusion.31
  711.8 17.9 %gather_fusion = bf16[250,128,128]{2,1,0:T(8,128)(2,1)} fusion(bf16[100,5,128,128]{3,2,1,0:T(8,128)(2,1)} %get-tuple-element.159, s32[250]{0:T(256)S(1)} %reshape.174), kind=kCustom, calls=%fused_computation.clone.1 | custom fusion | bytes 16386000 | tf_op jit(solution)/shard_map/while/body/eval_jaxpr/gather | solution.py:68
  729.8 12.8 %copy.65 = bf16[5,10,5,128,128]{3,4,1,2,0:T(8,128)(2,1)} copy(bf16[5,10,5,128,128]{4,3,2,1,0:T(8,128)(2,1)} %bitcast.50) | data formatting | bytes 16384000 | tf_op jit(solution)/shard_map/while/body/eval_jaxpr/gather | solution.py:68
  742.6 6.1 fusion.31
  752.6 256.4 %reduce-scatter.2.cloned.1.call-done = f32[5,5,128,128]{3,2,1,0:T(8,128)} async-done(((f32[40,5,128,128]{3,2,1,0:T(8,128)}), f32[5,5,128,128]{3,2,1,0:T(8,128)}) %reduce-scatter.2.cloned.1.call-update) | async-done | bytes 1638416 | tf_op jit(solution)/shard_map/reduce_scatter | solution.py:84
  (86 shorter events, 52.2 us)
Async XLA Ops:
  12.2 96.9 %all-to-all-start = ((bf16[8,5,5,128,128]{4,3,2,1,0:T(8,128)(2,1)}), bf16[8,5,5,128,128]{4,3,2,1,0:T(8,128)(2,1)}, u32[]{:S(2)}, u32[]{:S(2)}) async-start(bf16[8,5,5,128,128]{4,3,2,1,0:T(8,128)(2,1)} %stack.2), calls=%async_computation | async-start | bytes 13107200 | tf_op jit(solution)/shard_map/all_to_all | solution.py:29
  18.5 395.7 %all-reduce.4.cloned.1.call-start = ((), (), s32[]{:S(2)}) async-start(), calls=%async_computation.3 | async-start | bytes 26214400 | tf_op jit(solution)/shard_map/psum | solution.py:11
  117.4 0.7 copy-start
  117.5 891.5 %reduce-scatter.2.cloned.1.call-start = ((), (), s32[]{:S(2)}) async-start(), calls=%async_computation.2 | async-start | bytes 14745600 | tf_op jit(solution)/shard_map/reduce_scatter | solution.py:84
  751.8 0.7 copy-start.1
Sparse Core Ops, SparseCore 0:
  117.6 296.5 all-reduce.3
  752.0 256.9 reduce-scatter.1
